TPU v7x, 32 devices: a whole 2x2x4 slice. The times are simulated.
32 devices in a mesh: pairs: 8 (over z, x), vecs: 4 (over y, core).
Axes of the slice: x: 2, y: 2, z: 4, core: 2. Of those that a mesh axis runs over, the one named last changes fastest.
Arguments:
- prev_vectors: float32 [4096, 2048], P('pairs', 'vecs'), may hold values from -1 to 1
- columns: float32 [4096, 512], P('pairs'), may hold values from -20 to 200, as said below
- pivots: int32 [2, 256], replicated, may hold values from 0 to 4095, as said below
Outputs:
- new_vectors: float32 [4096, 512], P('pairs')
Inputs may be any that keep to these rules, and one draw needn't show every extreme that they name: All 2 x 256 pivots are distinct. The pivots of panel c lie in the c-th of 2 equal parts of the rows of each slab of 512 pairs. A slab holds at most 64 pivots of one panel, and in every panel some slab holds exactly 64. `columns`: in every panel the residual's pivot block is symmetric positive definite.
All inputs are finite; a program needn't handle non-finite values.
Results may differ from a plain program's by a relative error of at most 0.0001.
Values sent between devices are 32-bit elements; how exact they have to be, the bound alone decides.
A program may use at most 64 MiB of HBM per device.

v0:
```python
import jax
import jax.numpy as jnp
from jax import lax
from jax.sharding import PartitionSpec as P


def product(left, right):
    return jnp.dot(
        left, right.T, precision=lax.Precision.HIGHEST, preferred_element_type=jnp.float32
    )


def body(prev_vectors, columns, pivots):
    slab_rows = prev_vectors.shape[0]
    prev_width = prev_vectors.shape[1]
    panel_count = pivots.shape[0]
    panel_width = pivots.shape[1]
    shard_count = lax.axis_size("vecs")
    vec_index = lax.axis_index("vecs")
    quarter = panel_width // shard_count
    row_share = slab_rows // shard_count
    first_row = lax.axis_index("pairs") * slab_rows
    blocks = []
    for current in range(panel_count):
        pivot_ids = pivots[current]
        panel_columns = lax.slice_in_dim(
            columns, current * panel_width, (current + 1) * panel_width, axis=1
        )
        fresh_width = len(blocks) * quarter
        if blocks:
            fresh_local = jnp.concatenate(
                [
                    lax.dynamic_slice_in_dim(block, vec_index * quarter, quarter, 1)
                    for block in blocks
                ],
                axis=1,
            )
            sources = [prev_vectors, fresh_local, panel_columns]
        else:
            fresh_local = None
            sources = [prev_vectors, panel_columns]
        local_rows = pivot_ids - first_row
        owned_mask = (local_rows >= 0) & (local_rows < slab_rows)
        clipped = jnp.clip(local_rows, 0, slab_rows - 1)
        slot_most = max(1, 2 * panel_width // lax.axis_size("pairs"))
        owners = pivot_ids // slab_rows
        order_ids = jnp.arange(panel_width, dtype=jnp.int32)
        earlier = (owners[:, None] == owners[None, :]) & (order_ids[None, :] < order_ids[:, None])
        slot_rank = jnp.sum(earlier.astype(jnp.int32), axis=1)
        slot_ids = jnp.arange(slot_most, dtype=jnp.int32)
        slot_hit = (slot_rank[None, :] == slot_ids[:, None]) & owned_mask[None, :]
        slot_rows = jnp.sum(jnp.where(slot_hit, clipped[None, :], 0), axis=1)
        slot_live = jnp.any(slot_hit, axis=1)
        selected = jnp.concatenate(
            [jnp.where(slot_live[:, None], source[slot_rows], 0.0) for source in sources], axis=1
        )
        collected = lax.all_gather(selected, "pairs", axis=0, tiled=True)
        gathered = collected[owners * slot_most + slot_rank]
        prev_rows = gathered[:, :prev_width]
        fresh_rows = gathered[:, prev_width : prev_width + fresh_width]
        column_rows = gathered[:, prev_width + fresh_width :]
        gram_part = product(prev_rows, prev_rows)
        if blocks:
            gram_part = gram_part + product(fresh_rows, fresh_rows)
        gram = lax.psum(gram_part, "vecs")
        pivot_block = column_rows - gram
        symmetric = 0.5 * (pivot_block + pivot_block.T)
        factor = jnp.linalg.cholesky(symmetric)
        result = product(prev_vectors, prev_rows)
        if blocks:
            result = result + product(fresh_local, fresh_rows)
        summed = lax.psum_scatter(result, "vecs", scatter_dimension=0, tiled=True)
        own_columns = lax.dynamic_slice_in_dim(panel_columns, vec_index * row_share, row_share, 0)
        residual = own_columns - summed
        solved = jax.scipy.linalg.solve_triangular(factor, residual.T, lower=True)
        new_block = lax.all_gather(solved.T, "vecs", axis=0, tiled=True)
        blocks.append(new_block)
    return jnp.concatenate(blocks, axis=1)


def solution(mesh):
    placed = (P("pairs", "vecs"), P("pairs", None), P())
    return jax.shard_map(
        body, mesh=mesh, in_specs=placed, out_specs=P("pairs", None), check_vma=False
    )
```

profile of v0, /device:TPU:25, one launch (start us, length us, event | category | flops | bytes accessed | tf_op | source)
XLA Modules:
  0.0 327.4 jit_solution(9578203147786254027)
XLA Ops:
  6.5 0.8 fusion.37
  7.3 0.8 and_reduce_fusion.1
  8.1 1.3 fusion.36
  9.9 0.7 gather_fusion.1
  10.5 0.7 gather_fusion
  11.4 0.7 pad_maximum_fusion.2
  12.5 0.7 gather_fusion.3
  13.1 0.7 gather_fusion.5
  14.3 42.0 %all-gather.3.cloned.1.call-done = f32[512,768]{1,0:T(8,128)} async-done(((f32[64,768]{1,0:T(8,128)}), f32[512,768]{1,0:T(8,128)}) %all-gather.3.cloned.1.call-update) | async-done | bytes 1572880 | tf_op jit(solution)/shard_map/all_gather | solution.py:57
  56.2 2.8 gather_fusion.2
  59.0 1.3 fusion.4
  60.4 1.9 convolution_bitcast_fusion.1
  62.5 28.8 %all-reduce.4.cloned.1.call-done = f32[256,256]{1,0:T(8,128)} async-done(((f32[256,256]{1,0:T(8,128)}), f32[256,256]{1,0:T(8,128)}) %all-reduce.4.cloned.1.call-update) | async-done | bytes 262160 | tf_op jit(solution)/shard_map/psum | solution.py:65
  91.4 1.0 slice_subtract_fusion.1
  92.7 11.7 %cholesky.130 = f32[128,128]{1,0:T(8,128)S(1)} custom-call(f32[128,128]{1,0:T(8,128)S(1)} %cholesky.194), custom_call_target="Cholesky" | custom-call | tf_op jit(solution)/shard_map/jit(cholesky)/cholesky | solution.py:68
  104.5 9.8 %custom-call.13 = f32[1,128,128]{1,2,0:T(8,128)S(1)} custom-call(f32[1,128,128]{2,1,0:T(8,128)S(1)} %get-tuple-element.54), custom_call_target="InvertDiagBlocksLowerTriangular" | custom-call | tf_op jit(solution)/shard_map/jit(cholesky)/cholesky | solution.py:68
  114.8 11.7 %cholesky.147 = f32[128,128]{1,0:T(8,128)S(1)} custom-call(f32[128,128]{1,0:T(8,128)S(1)} %convolution_subtract_fusion.3), custom_call_target="Cholesky" | custom-call | tf_op jit(solution)/shard_map/jit(cholesky)/cholesky | solution.py:68
  126.5 0.7 compare_reduce_fusion.3
  127.3 0.7 compare_reduce_fusion.2
  129.3 4.3 %while.4 = (s32[]{:T(128)}, f32[256,256]{1,0:T(8,128)S(1)}, s32[2,2]{1,0:T(2,128)S(1)}, f32[2,128,128]{2,1,0:T(8,128)S(1)}, s32[]{:T(128)}) while((s32[]{:T(128)}, f32[256,256]{1,0:T(8,128)S(1)}, s32[2,2]{1,0:T(2,128)S(1)}, f32[2,128,128]{2,1,0:T(8,128)S(1)}, s32[]{:T(128)}) %tuple.51), condition=%wide.while_cond, body=%wide.while_body.sunk | while | flops 2 | bytes 131189 | solution.py:75
  129.6 0.7 fusion.51
  130.2 1.4 bitcast_dynamic-update-slice_fusion.4
  131.6 0.7 fusion.51
  132.3 1.4 bitcast_dynamic-update-slice_fusion.4
  133.6 19.7 %custom-call.14 = f32[2,128,128]{1,2,0:T(8,128)S(1)} custom-call(f32[2,128,128]{2,1,0:T(8,128)S(1)} %get-tuple-element.21), custom_call_target="InvertDiagBlocksLowerTriangular" | custom-call | tf_op jit(solution)/shard_map/jit(_solve_triangular)/triangular_solve | solution.py:75
  153.3 0.9 subtract_bitcast_fusion.1
  155.1 8.2 %all_gather.13 = f32[512,256]{0,1:T(8,128)S(1)} all-gather(f32[128,256]{0,1:T(8,128)S(1)} %maximum_bitcast_fusion), channel_id=1, replica_groups=mesh['pairs'=8,'vecs'=4] {'vecs'}, dimensions={0}, use_global_device_ids=true | all-gather | bytes 655360 | tf_op jit(solution)/shard_map/all_gather | solution.py:76
  164.1 0.8 pad_maximum_fusion.1
  165.1 45.4 %all-gather.5.cloned.1.call-done = f32[512,832]{1,0:T(8,128)} async-done(((f32[64,832]{1,0:T(8,128)}), f32[512,832]{1,0:T(8,128)}) %all-gather.5.cloned.1.call-update) | async-done | bytes 1703952 | tf_op jit(solution)/shard_map/all_gather | solution.py:57
  210.4 3.0 gather_fusion.6
  213.4 1.1 convolution_bitcast_fusion
  215.1 1.1 convolution_add_fusion.1
  216.5 1.4 convolution_add_fusion
  217.9 29.3 %all-reduce.6.cloned.1.call-done = f32[256,256]{1,0:T(8,128)} async-done(((f32[256,256]{1,0:T(8,128)}), f32[256,256]{1,0:T(8,128)}) %all-reduce.6.cloned.1.call-update) | async-done | bytes 262160 | tf_op jit(solution)/shard_map/psum | solution.py:65
  247.2 1.1 slice_subtract_fusion
  248.7 11.7 %cholesky.164 = f32[128,128]{1,0:T(8,128)S(1)} custom-call(f32[128,128]{1,0:T(8,128)S(1)} %cholesky.197), custom_call_target="Cholesky" | custom-call | tf_op jit(solution)/shard_map/jit(cholesky)/cholesky | solution.py:68
  260.5 9.8 %custom-call.15 = f32[1,128,128]{1,2,0:T(8,128)S(1)} custom-call(f32[1,128,128]{2,1,0:T(8,128)S(1)} %get-tuple-element.50), custom_call_target="InvertDiagBlocksLowerTriangular" | custom-call | tf_op jit(solution)/shard_map/jit(cholesky)/cholesky | solution.py:68
  270.8 11.7 %cholesky.181 = f32[128,128]{1,0:T(8,128)S(1)} custom-call(f32[128,128]{1,0:T(8,128)S(1)} %convolution_subtract_fusion.1), custom_call_target="Cholesky" | custom-call | tf_op jit(solution)/shard_map/jit(cholesky)/cholesky | solution.py:68
  282.5 0.7 compare_reduce_fusion.1
  285.2 4.4 %while.5 = (s32[]{:T(128)}, f32[256,256]{1,0:T(8,128)S(1)}, s32[2,2]{1,0:T(2,128)S(1)}, f32[2,128,128]{2,1,0:T(8,128)S(1)}, s32[]{:T(128)}) while((s32[]{:T(128)}, f32[256,256]{1,0:T(8,128)S(1)}, s32[2,2]{1,0:T(2,128)S(1)}, f32[2,128,128]{2,1,0:T(8,128)S(1)}, s32[]{:T(128)}) %tuple.69), condition=%wide.while_cond.clone, body=%wide.while_body.clone.sunk | while | flops 2 | bytes 131189 | solution.py:75
  285.5 0.7 fusion.52
  286.2 1.3 bitcast_dynamic-update-slice_fusion.5
  287.5 0.7 fusion.52
  288.2 1.3 bitcast_dynamic-update-slice_fusion.5
  289.6 19.7 %custom-call.16 = f32[2,128,128]{1,2,0:T(8,128)S(1)} custom-call(f32[2,128,128]{2,1,0:T(8,128)S(1)} %get-tuple-element.22), custom_call_target="InvertDiagBlocksLowerTriangular" | custom-call | tf_op jit(solution)/shard_map/jit(_solve_triangular)/triangular_solve | solution.py:75
  309.3 0.9 subtract_bitcast_fusion
  311.0 8.2 %all_gather.15 = f32[512,256]{0,1:T(8,128)S(1)} all-gather(f32[128,256]{0,1:T(8,128)S(1)} %maximum_bitcast_fusion.1), channel_id=1, replica_groups=mesh['pairs'=8,'vecs'=4] {'vecs'}, dimensions={0}, use_global_device_ids=true | all-gather | bytes 655360 | tf_op jit(solution)/shard_map/all_gather | solution.py:76
  319.2 1.3 copy.36
  (85 shorter events, 7.9 us)
Async XLA Ops:
  6.5 4.0 %copy-start = (f32[512,512]{1,0:T(8,128)S(1)}, f32[512,512]{1,0:T(8,128)}, u32[]{:S(2)}) copy-start(f32[512,512]{1,0:T(8,128)} %param.6) | copy-start | bytes 3145732
  6.5 49.7 %all-gather.3.cloned.1.call-start = ((), (), s32[]{:S(2)}) async-start(), calls=%async_computation.2 | async-start | bytes 1769472 | tf_op jit(solution)/shard_map/all_gather | solution.py:57
  11.2 2.7 copy-start.1
  12.1 79.3 %all-reduce.4.cloned.1.call-start = ((), (), s32[]{:S(2)}) async-start(), calls=%async_computation.3 | async-start | bytes 524288 | tf_op jit(solution)/shard_map/psum | solution.py:65
  60.4 93.0 %reduce-scatter.3.cloned.1.call-start = ((), (), s32[]{:S(2)}) async-start(), calls=%async_computation.4 | async-start | bytes 655360 | tf_op jit(solution)/shard_map/reduce_scatter | solution.py:72
  62.3 148.1 %all-gather.5.cloned.1.call-start = ((), (), s32[]{:S(2)}) async-start(), calls=%async_computation.5 | async-start | bytes 2064384 | tf_op jit(solution)/shard_map/all_gather | solution.py:57
  164.9 82.4 %all-reduce.6.cloned.1.call-start = ((), (), s32[]{:S(2)}) async-start(), calls=%async_computation.6 | async-start | bytes 524288 | tf_op jit(solution)/shard_map/psum | solution.py:65
  216.2 93.0 %reduce-scatter.5.cloned.1.call-start = ((), (), s32[]{:S(2)}) async-start(), calls=%async_computation.7 | async-start | bytes 655360 | tf_op jit(solution)/shard_map/reduce_scatter | solution.py:72
Sparse Core Ops, SparseCore 0:
  12.2 43.9 all-gather.2
  60.5 30.8 all-reduce.3
  94.0 22.9 reduce-scatter.2
  165.0 45.3 all-gather.4
  216.3 30.8 all-reduce.5
  249.7 22.9 reduce-scatter.4
where the time goes:
time: 329 us; the launch traced here: 327 us
  waiting for transfers between devices  146 us (44%)
  other arithmetic  117 us (36%)
  local copies, waits for them, and re-layouts  20.7 us (6%)
  between operations  16.5 us (5%)
  blocking collectives  16.3 us (5%)
  matrix products  9.76 us (3%)
    all_gather x2, waiting for transfers between devices, body(): collected = lax.all_gather(selected, 'pairs', axis=0, tiled=True)  87.3 us
    another operation x14, other arithmetic, body(): factor = jnp.linalg.cholesky(symmetric)  69.3 us
    psum x2, waiting for transfers between devices, body(): gram = lax.psum(gram_part, 'vecs')  58.2 us
    another operation x5, other arithmetic, body(): solved = jax.scipy.linalg.solve_triangular(factor, residual.T, lower=True)  39.4 us
    all_gather x2, blocking collectives, body(): new_block = lax.all_gather(solved.T, 'vecs', axis=0, tiled=True)  16.3 us
    another operation x15, local copies, waits for them, and re-layouts, body(): solved = jax.scipy.linalg.solve_triangular(factor, residual.T, lower=True)  8.16 us
    dot_general x6, matrix products, product(): jnp.dot(left, right.T, precision=lax.Precision.HIGHEST, preferred_element...  7.27 us
  transfers between devices with their start and end apart: 6, of which 4 were waited for; matrix products, arithmetic and copies ran while one was open for 38% of the time, Pallas kernels for 0%

commit v1 on v0

v1 whole, which is shorter than its diff:
```python
import functools

import jax
import jax.numpy as jnp
from jax import lax
from jax.experimental import pallas as pl
from jax.experimental.pallas import tpu as pltpu
from jax.sharding import PartitionSpec as P

F32 = jnp.float32
BF16 = jnp.bfloat16
STEP = 16


def split2(x):
    high = x.astype(BF16)
    return high, (x - high.astype(F32)).astype(BF16)


def split3(x):
    high = x.astype(BF16)
    rest = x - high.astype(F32)
    mid = rest.astype(BF16)
    return high, mid, (rest - mid.astype(F32)).astype(BF16)


def dot(a, b, dims):
    return lax.dot_general(a, b, (dims, ((), ())), preferred_element_type=F32)


def dot_nt(a, b):
    nt = ((1,), (1,))
    return dot(a[0], b[0], nt) + (dot(a[0], b[1], nt) + dot(a[1], b[0], nt))


def eliminate(work, inverse, chunk, chunks):
    size = work.shape[0]
    per = size // chunks
    first = chunk * per
    lane0 = first // 128 * 128
    lane1 = size + -(-(first + per) // 128) * 128
    row_ids = lax.broadcasted_iota(jnp.int32, (STEP, 128), 0)

    def group(g, _):
        row = pl.multiple_of(g * STEP, STEP)
        band = work[pl.ds(row, STEP), lane0:lane1]
        shift = lax.rem(128 - lax.rem(row, 128), 128)
        near = pltpu.roll(band[:, :128], shift, 1)
        cols = [jnp.broadcast_to(near[:, j : j + 1], (STEP, 128)) for j in range(STEP)]
        tiles = [band[:, t : t + 128] for t in range(0, lane1 - lane0, 128)]
        diag = jnp.ones((STEP, 128), F32)
        for k in range(STEP):
            pivot = cols[k][k : k + 1, :]
            diag = jnp.where(row_ids == k, pivot, diag)
            if k == STEP - 1:
                break
            mult = jnp.where(row_ids > k, cols[k] * (1.0 / pivot), 0.0)
            for j in range(k + 1, STEP):
                cols[j] = cols[j] - mult * cols[j][k : k + 1, :]
            tiles = [t - mult * t[k : k + 1, :] for t in tiles]
        scale = lax.rsqrt(diag)
        band = jnp.concatenate([t * scale for t in tiles], axis=1)
        inverse[pl.ds(row, STEP), : lane1 - size] = band[:, size - lane0 :]
        h, m, l = split3(band)
        left = jnp.concatenate([h, h, m, h, l, m], axis=0)[:, first - lane0 : size - lane0]
        right = jnp.concatenate([h, m, h, l, h, m], axis=0)
        work[first:, lane0:lane1] = work[first:, lane0:lane1] - dot(left, right, ((0,), (0,)))
        return 0

    lax.fori_loop(first // STEP, (first + per) // STEP, group, 0)


def set_work(work, inverse, symmetric):
    size = symmetric.shape[0]
    rows = lax.broadcasted_iota(jnp.int32, (size, size), 0)
    lanes = lax.broadcasted_iota(jnp.int32, (size, size), 1)
    work[:, :size] = symmetric
    work[:, size:] = jnp.where(rows == lanes, 1.0, 0.0).astype(F32)
    inverse[...] = jnp.zeros_like(inverse)


def kernel(
    pair_count, sent_ref, pos_ref, prev_ref, cols_ref, out_ref,
    table, p_high, p_low,
    x1, a1, b1, f1, x2, a2, b2, f2, x3, a3, b3, f3,
    work1, inv1, work2, inv2,
    z_send, z_recv, x_send, x_recv, r_send, r_recv,
):
    panels, slots, _ = sent_ref.shape
    depth = prev_ref.shape[1]
    width = cols_ref.shape[1] // panels
    outer = pair_count // 2
    me = lax.axis_index("pairs")
    vec = lax.axis_index("vecs")
    zi, xi = me // 2, lax.rem(me, 2)
    vy, vc = vec // 2, lax.rem(vec, 2)
    x_peer = {"pairs": zi * 2 + 1 - xi}
    c_peer = {"vecs": vy * 2 + 1 - vc}
    y_peer = {"vecs": (1 - vy) * 2 + vc}
    z_peers = [{"pairs": lax.rem(zi + d, outer) * 2 + xi} for d in range(1, outer)]
    mesh_id = pl.DeviceIdType.MESH

    barrier = pltpu.get_barrier_semaphore()
    everyone = [x_peer, c_peer, y_peer] + z_peers
    for peer in everyone:
        pl.semaphore_signal(barrier, inc=1, device_id=peer, device_id_type=mesh_id)
    pl.semaphore_wait(barrier, len(everyone))

    def rows_of(z, x):
        return pl.ds(pl.multiple_of((z * 2 + x) * slots, slots), slots)

    def z_copy(c, d):
        return pltpu.make_async_remote_copy(
            src_ref=sent_ref.at[c], dst_ref=table.at[c, rows_of(zi, xi)],
            send_sem=z_send.at[c, d], recv_sem=z_recv.at[c, d],
            device_id=z_peers[d - 1], device_id_type=mesh_id,
        )

    def z_arrival(c, d):
        return pltpu.make_async_remote_copy(
            src_ref=sent_ref.at[c], dst_ref=table.at[c, rows_of(lax.rem(zi + outer - d, outer), xi)],
            send_sem=z_send.at[c, d], recv_sem=z_recv.at[c, d],
            device_id=z_peers[d - 1], device_id_type=mesh_id,
        )

    def x_copy(c, d):
        rows = rows_of(lax.rem(zi + outer - d, outer), xi)
        return pltpu.make_async_remote_copy(
            src_ref=sent_ref.at[c] if d == 0 else table.at[c, rows], dst_ref=table.at[c, rows],
            send_sem=x_send.at[c, d], recv_sem=x_recv.at[c, d],
            device_id=x_peer, device_id_type=mesh_id,
        )

    def x_arrival(c, d):
        rows = rows_of(lax.rem(zi + outer - d, outer), 1 - xi)
        return pltpu.make_async_remote_copy(
            src_ref=sent_ref.at[c], dst_ref=table.at[c, rows],
            send_sem=x_send.at[c, d], recv_sem=x_recv.at[c, d],
            device_id=x_peer, device_id_type=mesh_id,
        )

    def forward(c):
        for d in range(1, outer):
            z_arrival(c, d).wait_recv()
            x_copy(c, d).start()

    def finish_gather(c):
        for d in range(outer):
            x_arrival(c, d).wait_recv()

    def half(ref, which):
        count = ref.shape[0] // 2
        return ref.at[pl.ds(pl.multiple_of(which * count, count), count)]

    def exchange(src, dst, n, stage, peer):
        return pltpu.make_async_remote_copy(
            src_ref=src, dst_ref=dst, send_sem=r_send.at[n, stage], recv_sem=r_recv.at[n, stage],
            device_id=peer, device_id_type=mesh_id,
        )

    def stage_a(n, x, a):
        return exchange(half(x, 1 - vc), a, n, 0, c_peer)

    def stage_b(n, x, b):
        return exchange(half(x, vc), b, n, 1, y_peer)

    def stage_c(n, f):
        return exchange(half(f, vc), half(f, vc), n, 2, c_peer)

    def stage_c_arrival(n, f):
        return exchange(half(f, 1 - vc), half(f, 1 - vc), n, 2, c_peer)

    def a_to_b(n, x, a, b):
        stage_a(n, x, a).wait_recv()
        own = half(x, vc)
        own[...] = own[...] + a[...]
        stage_b(n, x, b).start()

    def b_to_c(n, x, b, f):
        stage_b(n, x, b).wait_recv()
        half(f, vc)[...] = half(x, vc)[...] + b[...]
        stage_c(n, f).start()

    for c in range(panels):
        for d in range(1, outer):
            z_copy(c, d).start()
        if c == 0:
            x_copy(c, 0).start()
    for c in range(1, panels):
        x_copy(c, 0).start()
    for c in range(panels):
        table[c, rows_of(zi, xi)] = sent_ref[c]

    quarter = cols_ref.shape[1] // 4

    def ordered(c):
        place = pos_ref[c]
        count = pair_count * slots
        hit = lax.broadcasted_iota(jnp.int32, (width, count), 1) == place
        pick = jnp.where(hit, 1.0, 0.0).astype(BF16)
        nn = ((1,), (0,))
        high, low = split2(table[c, :, :depth])
        p_high[c] = dot(pick, high, nn).astype(BF16)
        p_low[c] = dot(pick, low, nn).astype(BF16)
        th, tm, tl = split3(table[c, :, depth:])
        return dot(pick, th, nn) + dot(pick, tm, nn) + dot(pick, tl, nn)

    def place_share(share, lanes):
        tiles = []
        for q in range(lanes // quarter):
            tiles.append(jnp.where(vec == q, share, 0.0))
        return jnp.concatenate(tiles, axis=1)

    forward(0)
    finish_gather(0)
    share = ordered(0)
    rows0 = (p_high[0], p_low[0])
    x1[...] = place_share(share, width) - dot_nt(rows0, rows0)
    stage_a(0, x1, a1).start()
    a_to_b(0, x1, a1, b1)
    forward(1)
    b_to_c(0, x1, b1, f1)
    stage_c_arrival(0, f1).wait_recv()

    block = f1[...]
    set_work(work1, inv1, 0.5 * (block + block.T))
    eliminate(work1, inv1, 0, 4)

    finish_gather(1)
    share = ordered(1)
    rows0 = (p_high[0], p_low[0])
    rows1 = (p_high[1], p_low[1])
    known = jnp.concatenate([dot_nt(rows1, rows0), dot_nt(rows1, rows1)], axis=1)
    x2[...] = place_share(share, 2 * width) - known
    stage_a(1, x2, a2).start()
    own = split2(prev_ref[...])
    x3[:, :width] = dot_nt(own, rows0)
    x3[:, width:] = dot_nt(own, rows1)
    stage_a(2, x3, a3).start()
    a_to_b(1, x2, a2, b2)
    eliminate(work1, inv1, 1, 4)
    a_to_b(2, x3, a3, b3)
    eliminate(work1, inv1, 2, 4)
    b_to_c(1, x2, b2, f2)
    eliminate(work1, inv1, 3, 4)
    stage_c_arrival(1, f2).wait_recv()

    inverse1 = split2(inv1[...])
    cross = split2(dot_nt(split2(f2[:, :width]), inverse1))
    block = f2[:, width:] - dot_nt(cross, cross)
    set_work(work2, inv2, 0.5 * (block + block.T))
    eliminate(work2, inv2, 0, 4)
    eliminate(work2, inv2, 1, 4)
    b_to_c(2, x3, b3, f3)
    eliminate(work2, inv2, 2, 4)
    stage_c_arrival(2, f3).wait_recv()
    new1 = dot_nt(split2(cols_ref[:, :width] - f3[:, :width]), inverse1)
    out_ref[:, :width] = new1
    rest = cols_ref[:, width:] - f3[:, width:] - dot_nt(split2(new1), cross)
    eliminate(work2, inv2, 3, 4)
    out_ref[:, width:] = dot_nt(split2(rest), split2(inv2[...]))

    for c in range(panels):
        for d in range(1, outer):
            z_copy(c, d).wait_send()
        for d in range(outer):
            x_copy(c, d).wait_send()
    for n, (x, a, b, f) in enumerate(((x1, a1, b1, f1), (x2, a2, b2, f2), (x3, a3, b3, f3))):
        stage_a(n, x, a).wait_send()
        stage_b(n, x, b).wait_send()
        stage_c(n, f).wait_send()


def body(prev_vectors, columns, pivots):
    slab_rows, depth = prev_vectors.shape
    panels, width = pivots.shape
    pair_count = lax.axis_size("pairs")
    slots = max(8, 2 * width // pair_count)
    me = lax.axis_index("pairs")
    vec = lax.axis_index("vecs")
    owners = pivots // slab_rows
    order = jnp.arange(width, dtype=jnp.int32)
    earlier = (owners[:, :, None] == owners[:, None, :]) & (order[None, None, :] < order[None, :, None])
    rank = jnp.sum(earlier.astype(jnp.int32), axis=2)
    place = owners * slots + rank
    wanted = me * slots + jnp.arange(slots, dtype=jnp.int32)
    hit = place[:, None, :] == wanted[None, :, None]
    local = jnp.sum(jnp.where(hit, (pivots - me * slab_rows)[:, None, :], 0), axis=2).reshape(-1)
    quarter = columns.shape[1] // lax.axis_size("vecs")
    share = lax.dynamic_slice_in_dim(columns, vec * quarter, quarter, 1)
    sent = jnp.concatenate([prev_vectors[local], share[local]], axis=1)
    sent = sent.reshape(panels, slots, depth + quarter)
    count = pair_count * slots
    outer = pair_count // 2

    def vmem(*shape, dtype=F32):
        return pltpu.VMEM(shape, dtype)

    def reduced(rows, lanes):
        return [vmem(rows, lanes), vmem(rows // 2, lanes), vmem(rows // 2, lanes), vmem(rows, lanes)]

    scratch = [
        vmem(panels, count, depth + quarter),
        vmem(panels, width, depth, dtype=BF16),
        vmem(panels, width, depth, dtype=BF16),
        *reduced(width, width),
        *reduced(width, 2 * width),
        *reduced(slab_rows, 2 * width),
        vmem(width, 2 * width), vmem(width, width),
        vmem(width, 2 * width), vmem(width, width),
        pltpu.SemaphoreType.DMA((panels, outer)),
        pltpu.SemaphoreType.DMA((panels, outer)),
        pltpu.SemaphoreType.DMA((panels, outer)),
        pltpu.SemaphoreType.DMA((panels, outer)),
        pltpu.SemaphoreType.DMA((3, 3)),
        pltpu.SemaphoreType.DMA((3, 3)),
    ]
    whole = pl.BlockSpec(memory_space=pltpu.VMEM)
    return pl.pallas_call(
        functools.partial(kernel, pair_count),
        out_shape=jax.ShapeDtypeStruct((slab_rows, panels * width), F32),
        in_specs=[whole] * 4,
        out_specs=whole,
        scratch_shapes=scratch,
        compiler_params=pltpu.CompilerParams(
            collective_id=0, has_side_effects=True, vmem_limit_bytes=48 * 1024 * 1024
        ),
    )(sent, place[:, :, None], prev_vectors, columns)


def solution(mesh):
    placed = (P("pairs", "vecs"), P("pairs", None), P())
    return jax.shard_map(
        body, mesh=mesh, in_specs=placed, out_specs=P("pairs", None), check_vma=False
    )
```

time: 329 us -> 79.3 us (0.24)
  waiting for transfers between devices: 146 us -> 0 us
  other arithmetic: 117 us -> 1.29 us
  Pallas kernels: 0 us -> 73.5 us
  local copies, waits for them, and re-layouts: 20.7 us -> 4.01 us
  between operations: 16.5 us -> 0.06 us
  blocking collectives: 16.3 us -> 0 us
  matrix products: 9.76 us -> 0 us
    another operation x19 -> x0, other arithmetic: 109 us -> none  [the longest x14 69.3 us: body(): factor = jnp.linalg.cholesky(symmetric)]
    all_gather x2 -> x0, waiting for transfers between devices: 87.3 us -> none  [body(): collected = lax.all_gather(selected, 'pairs', axis=0, tiled=True)]
    pallas_call x0 -> x1, Pallas kernels: none -> 73.5 us  [body(): pl.pallas_call(functools.partial(kernel, pair_count), out_shape=jax.Shape...]
    psum x2 -> x0, waiting for transfers between devices: 58.2 us -> none  [body(): gram = lax.psum(gram_part, 'vecs')]
    all_gather x2 -> x0, blocking collectives: 16.3 us -> none  [body(): new_block = lax.all_gather(solved.T, 'vecs', axis=0, tiled=True)]
    another operation x19 -> x0, local copies, waits for them, and re-layouts: 8.21 us -> none  [the longest x15 8.16 us: body(): solved = jax.scipy.linalg.solve_triangular(factor, residual.T, lower=True)]
    gather x7 -> x2, local copies, waits for them, and re-layouts: 9.02 us -> 1.4 us  [body(): sent = jnp.concatenate([prev_vectors[local], share[local]], axis=1)]
    dot_general x6 -> x0, matrix products: 7.27 us -> none  [product(): jnp.dot(left, right.T, precision=lax.Precision.HIGHEST, preferred_element...]
  transfers between devices with their start and end apart: 6 -> 0, of which waited for: 4 -> 0; matrix products, arithmetic and copies ran while one was open for 38% -> 0% of each run, Pallas kernels for 0% -> 0%
where the time goes in v1:
time: 79.3 us; the launch traced here: 78.9 us
  Pallas kernels  73.5 us (93%)
  local copies, waits for them, and re-layouts  4.01 us (5%)
  other arithmetic  1.29 us (2%)
    pallas_call x1, Pallas kernels, body(): pl.pallas_call(functools.partial(kernel, pair_count), out_shape=jax.Shape...  73.5 us

profile of v1, /device:TPU:25, one launch (start us, length us, event | category | flops | bytes accessed | tf_op | source)
XLA Modules:
  0.0 78.9 jit_solution(12573121836459717901)
XLA Ops:
  0.0 0.0 copy-start
  0.0 0.8 and_select_fusion
  0.8 0.2 convert_reduce_fusion
  1.1 0.2 select_reduce_fusion
  1.3 0.1 reshape.57
  1.4 0.1 copy.5.pos_ref
  1.5 1.0 %constant_dynamic-slice_fusion = f32[512,128]{1,0:T(8,128)S(1)} fusion(f32[512,512]{1,0:T(8,128)} %cols_ref.1, s32[]{:T(128)S(6)} %select_n.26), kind=kLoop, calls=%fused_computation.16 | loop fusion | bytes 524292 | tf_op jit(solution)/shard_map/dynamic_slice | solution.py:290
  2.5 0.6 gather_fusion.1
  3.1 0.0 copy-done
  3.1 0.0 copy-start.1
  3.2 0.8 gather_fusion
  4.0 0.4 copy-done.1
  4.4 73.5 %shard_map.37 = f32[512,512]{1,0:T(8,128)S(1)} custom-call(f32[2,64,640]{2,1,0:T(8,128)S(1)} %bitcast.4, s32[2,256,1]{2,1,0:T(8,128)S(1)} %copy.5.pos_ref, f32[512,512]{1,0:T(8,128)S(1)} %copy-done, f32[512,512]{1,0:T(8,128)S(1)} %copy-done.1), custom_call_target="tpu_custom_call" | custom-call | tf_op jit(solution)/shard_map/pallas_call | solution.py:319
  77.9 1.0 %copy.7 = f32[512,512]{1,0:T(8,128)} copy(f32[512,512]{1,0:T(8,128)S(1)} %shard_map.37) | data formatting | bytes 2097152
  (6 shorter events, 0.1 us)
Async XLA Ops:
  0.0 3.1 %copy-start = (f32[512,512]{1,0:T(8,128)S(1)}, f32[512,512]{1,0:T(8,128)}, u32[]{:S(2)}) copy-start(f32[512,512]{1,0:T(8,128)} %prev_ref.1) | copy-start | bytes 3145732
  3.1 1.2 %copy-start.1 = (f32[512,512]{1,0:T(8,128)S(1)}, f32[512,512]{1,0:T(8,128)}, u32[]{:S(2)}) copy-start(f32[512,512]{1,0:T(8,128)} %cols_ref.1) | copy-start | bytes 3145732

commit v2 on v1

--- a/solution.py
+++ b/solution.py
@@ -33,21 +33,25 @@
     return dot(a[0], b[0], nt) + (dot(a[0], b[1], nt) + dot(a[1], b[0], nt))
 
 
-def eliminate(work, inverse, chunk, chunks):
+def live_tiles(size, row):
+    return range(row // 128, size // 128 + row // 128 + 1)
+
+
+def start_band(work):
+    return {t: work[:STEP, t * 128 : t * 128 + 128] for t in live_tiles(work.shape[0], 0)}
+
+
+def eliminate(work, inverse, chunk, chunks, band):
     size = work.shape[0]
-    per = size // chunks
-    first = chunk * per
-    lane0 = first // 128 * 128
-    lane1 = size + -(-(first + per) // 128) * 128
+    parts = size // 128
+    per = size // STEP // chunks
     row_ids = lax.broadcasted_iota(jnp.int32, (STEP, 128), 0)
-
-    def group(g, _):
-        row = pl.multiple_of(g * STEP, STEP)
-        band = work[pl.ds(row, STEP), lane0:lane1]
-        shift = lax.rem(128 - lax.rem(row, 128), 128)
-        near = pltpu.roll(band[:, :128], shift, 1)
-        cols = [jnp.broadcast_to(near[:, j : j + 1], (STEP, 128)) for j in range(STEP)]
-        tiles = [band[:, t : t + 128] for t in range(0, lane1 - lane0, 128)]
+    for g in range(chunk * per, (chunk + 1) * per):
+        row = g * STEP
+        lane = row % 128
+        names = live_tiles(size, row)
+        tiles = [band[t] for t in names]
+        cols = [jnp.broadcast_to(tiles[0][:, lane + j : lane + j + 1], (STEP, 128)) for j in range(STEP)]
         diag = jnp.ones((STEP, 128), F32)
         for k in range(STEP):
             pivot = cols[k][k : k + 1, :]
@@ -59,15 +63,29 @@
                 cols[j] = cols[j] - mult * cols[j][k : k + 1, :]
             tiles = [t - mult * t[k : k + 1, :] for t in tiles]
         scale = lax.rsqrt(diag)
-        band = jnp.concatenate([t * scale for t in tiles], axis=1)
-        inverse[pl.ds(row, STEP), : lane1 - size] = band[:, size - lane0 :]
-        h, m, l = split3(band)
-        left = jnp.concatenate([h, h, m, h, l, m], axis=0)[:, first - lane0 : size - lane0]
+        tiles = [t * scale for t in tiles]
+        for t, tile in zip(names, tiles):
+            if t >= parts:
+                inverse[row : row + STEP, (t - parts) * 128 : (t - parts) * 128 + 128] = tile
+        after = row + STEP
+        if after == size:
+            return None
+        lane0 = names[0] * 128
+        lane1 = lane0 + 128 * len(tiles)
+        h, m, l = split3(jnp.concatenate(tiles, axis=1))
+        left = jnp.concatenate([h, h, m, h, l, m], axis=0)
         right = jnp.concatenate([h, m, h, l, h, m], axis=0)
-        work[first:, lane0:lane1] = work[first:, lane0:lane1] - dot(left, right, ((0,), (0,)))
-        return 0
-
-    lax.fori_loop(first // STEP, (first + per) // STEP, group, 0)
+        near = dot(left[:, after - lane0 : after + STEP - lane0], right, ((0,), (0,)))
+        band = {}
+        for t in live_tiles(size, after):
+            band[t] = work[after : after + STEP, t * 128 : t * 128 + 128]
+            if t in names:
+                band[t] = band[t] - near[:, t * 128 - lane0 : t * 128 - lane0 + 128]
+        rest = after + STEP
+        if rest < size:
+            far = dot(left[:, rest - lane0 : size - lane0], right, ((0,), (0,)))
+            work[rest:, lane0:lane1] = work[rest:, lane0:lane1] - far
+    return band
 
 
 def set_work(work, inverse, symmetric):
@@ -181,13 +199,12 @@
         half(f, vc)[...] = half(x, vc)[...] + b[...]
         stage_c(n, f).start()
 
-    for c in range(panels):
+    def begin(c):
         for d in range(1, outer):
             z_copy(c, d).start()
-        if c == 0:
-            x_copy(c, 0).start()
-    for c in range(1, panels):
         x_copy(c, 0).start()
+
+    begin(0)
     for c in range(panels):
         table[c, rows_of(zi, xi)] = sent_ref[c]
 
@@ -212,6 +229,7 @@
         return jnp.concatenate(tiles, axis=1)
 
     forward(0)
+    begin(1)
     finish_gather(0)
     share = ordered(0)
     rows0 = (p_high[0], p_low[0])
@@ -224,7 +242,7 @@
 
     block = f1[...]
     set_work(work1, inv1, 0.5 * (block + block.T))
-    eliminate(work1, inv1, 0, 4)
+    band = eliminate(work1, inv1, 0, 4, start_band(work1))
 
     finish_gather(1)
     share = ordered(1)
@@ -238,26 +256,26 @@
     x3[:, width:] = dot_nt(own, rows1)
     stage_a(2, x3, a3).start()
     a_to_b(1, x2, a2, b2)
-    eliminate(work1, inv1, 1, 4)
+    band = eliminate(work1, inv1, 1, 4, band)
     a_to_b(2, x3, a3, b3)
-    eliminate(work1, inv1, 2, 4)
+    band = eliminate(work1, inv1, 2, 4, band)
     b_to_c(1, x2, b2, f2)
-    eliminate(work1, inv1, 3, 4)
+    band = eliminate(work1, inv1, 3, 4, band)
     stage_c_arrival(1, f2).wait_recv()
 
     inverse1 = split2(inv1[...])
     cross = split2(dot_nt(split2(f2[:, :width]), inverse1))
     block = f2[:, width:] - dot_nt(cross, cross)
     set_work(work2, inv2, 0.5 * (block + block.T))
-    eliminate(work2, inv2, 0, 4)
-    eliminate(work2, inv2, 1, 4)
+    band = eliminate(work2, inv2, 0, 4, start_band(work2))
+    band = eliminate(work2, inv2, 1, 4, band)
     b_to_c(2, x3, b3, f3)
-    eliminate(work2, inv2, 2, 4)
+    band = eliminate(work2, inv2, 2, 4, band)
     stage_c_arrival(2, f3).wait_recv()
     new1 = dot_nt(split2(cols_ref[:, :width] - f3[:, :width]), inverse1)
     out_ref[:, :width] = new1
     rest = cols_ref[:, width:] - f3[:, width:] - dot_nt(split2(new1), cross)
-    eliminate(work2, inv2, 3, 4)
+    band = eliminate(work2, inv2, 3, 4, band)
     out_ref[:, width:] = dot_nt(split2(rest), split2(inv2[...]))
 
     for c in range(panels):
@@ -278,7 +296,7 @@
     slots = max(8, 2 * width // pair_count)
     me = lax.axis_index("pairs")
     vec = lax.axis_index("vecs")
-    owners = pivots // slab_rows
+    owners = lax.div(pivots, jnp.int32(slab_rows))
     order = jnp.arange(width, dtype=jnp.int32)
     earlier = (owners[:, :, None] == owners[:, None, :]) & (order[None, None, :] < order[None, :, None])
     rank = jnp.sum(earlier.astype(jnp.int32), axis=2)
@@ -287,8 +305,8 @@
     hit = place[:, None, :] == wanted[None, :, None]
     local = jnp.sum(jnp.where(hit, (pivots - me * slab_rows)[:, None, :], 0), axis=2).reshape(-1)
     quarter = columns.shape[1] // lax.axis_size("vecs")
-    share = lax.dynamic_slice_in_dim(columns, vec * quarter, quarter, 1)
-    sent = jnp.concatenate([prev_vectors[local], share[local]], axis=1)
+    share = lax.dynamic_slice_in_dim(columns[local], vec * quarter, quarter, 1)
+    sent = jnp.concatenate([prev_vectors[local], share], axis=1)
     sent = sent.reshape(panels, slots, depth + quarter)
     count = pair_count * slots
     outer = pair_count // 2

time: 79.3 us -> 78.3 us (0.987)
  Pallas kernels: 73.5 us -> 72.2 us
  local copies, waits for them, and re-layouts: 4.01 us -> 5.28 us
    gather x2, local copies, waits for them, and re-layouts: 1.4 us -> 2.94 us  [the longest x1 2.19 us: body(): share = lax.dynamic_slice_in_dim(columns[local], vec * quarter, quarter, 1)]
    pallas_call x1, Pallas kernels: 73.5 us -> 72.2 us  [body(): pl.pallas_call(functools.partial(kernel, pair_count), out_shape=jax.Shape...]
    dynamic_slice x1, local copies, waits for them, and re-layouts: 0.98 us -> 0.02 us  [body(): share = lax.dynamic_slice_in_dim(columns[local], vec * quarter, quarter, 1)]
    unnamed x5 -> x7, local copies, waits for them, and re-layouts: 1.4 us -> 2.08 us
where the time goes in v2:
time: 78.3 us; the launch traced here: 78.1 us
  Pallas kernels  72.2 us (92%)
  local copies, waits for them, and re-layouts  5.28 us (7%)
    pallas_call x1, Pallas kernels, body(): pl.pallas_call(functools.partial(kernel, pair_count), out_shape=jax.Shape...  72.2 us
    gather x1, local copies, waits for them, and re-layouts, body(): share = lax.dynamic_slice_in_dim(columns[local], vec * quarter, quarter, 1)  2.19 us
    unnamed x7, local copies, waits for them, and re-layouts  2.08 us

profile of v2, /device:TPU:25, one launch (start us, length us, event | category | flops | bytes accessed | tf_op | source)
XLA Modules:
  0.0 78.1 jit_solution(8991682498613838921)
XLA Ops:
  0.0 0.0 copy-start.2
  0.0 0.7 copy-done.2
  0.7 0.2 convert_reduce_fusion
  1.0 0.2 select_reduce_fusion
  1.2 0.1 reshape.57
  1.3 0.1 copy.5.pos_ref
  1.4 0.0 copy-start.1
  1.4 2.2 %gather_fusion.1 = f32[128,512]{1,0:T(8,128)S(1)} fusion(f32[512,512]{1,0:T(8,128)} %cols_ref.1, s32[1024]{0:T(1024)S(1)} %pad_clamp_fusion), kind=kCustom, calls=%fused_computation.1 | custom fusion | bytes 524800 | tf_op jit(solution)/shard_map/gather | solution.py:308
  3.7 0.0 copy-done.1
  3.7 0.0 copy-start
  3.7 0.8 gather_fusion
  4.5 0.4 copy-done
  4.9 72.2 %shard_map.41 = f32[512,512]{1,0:T(8,128)S(1)} custom-call(f32[2,64,640]{2,1,0:T(8,128)S(1)} %bitcast.4, s32[2,256,1]{2,1,0:T(8,128)S(1)} %copy.5.pos_ref, f32[512,512]{1,0:T(8,128)S(1)} %copy-done.1, f32[512,512]{1,0:T(8,128)S(1)} %copy-done), custom_call_target="tpu_custom_call" | custom-call | tf_op jit(solution)/shard_map/pallas_call | solution.py:337
  77.1 1.0 %copy.7 = f32[512,512]{1,0:T(8,128)} copy(f32[512,512]{1,0:T(8,128)S(1)} %shard_map.41) | data formatting | bytes 2097152
  (8 shorter events, 0.1 us)
Async XLA Ops:
  0.0 0.7 copy-start.2
  1.4 2.2 %copy-start.1 = (f32[512,512]{1,0:T(8,128)S(1)}, f32[512,512]{1,0:T(8,128)}, u32[]{:S(2)}) copy-start(f32[512,512]{1,0:T(8,128)} %prev_ref.1) | copy-start | bytes 3145732
  3.7 1.2 %copy-start = (f32[512,512]{1,0:T(8,128)S(1)}, f32[512,512]{1,0:T(8,128)}, u32[]{:S(2)}) copy-start(f32[512,512]{1,0:T(8,128)} %cols_ref.1) | copy-start | bytes 3145732

commit v3 on v2

--- a/solution.py
+++ b/solution.py
@@ -39,6 +39,12 @@
 
 def start_band(work):
     return {t: work[:STEP, t * 128 : t * 128 + 128] for t in live_tiles(work.shape[0], 0)}
+
+
+def inverse_of(x):
+    guess = pl.reciprocal(x, approx=True)
+    guess = guess * (2.0 - x * guess)
+    return guess * (2.0 - x * guess)
 
 
 def eliminate(work, inverse, chunk, chunks, band):
@@ -53,15 +59,25 @@
         tiles = [band[t] for t in names]
         cols = [jnp.broadcast_to(tiles[0][:, lane + j : lane + j + 1], (STEP, 128)) for j in range(STEP)]
         diag = jnp.ones((STEP, 128), F32)
-        for k in range(STEP):
-            pivot = cols[k][k : k + 1, :]
-            diag = jnp.where(row_ids == k, pivot, diag)
-            if k == STEP - 1:
-                break
-            mult = jnp.where(row_ids > k, cols[k] * (1.0 / pivot), 0.0)
-            for j in range(k + 1, STEP):
-                cols[j] = cols[j] - mult * cols[j][k : k + 1, :]
-            tiles = [t - mult * t[k : k + 1, :] for t in tiles]
+        for k in range(0, STEP, 2):
+            p, q = cols[k], cols[k + 1]
+            a, b, c = p[k : k + 1, :], p[k + 1 : k + 2, :], q[k + 1 : k + 2, :]
+            over_a = inverse_of(a)
+            over_det = inverse_of(a * c - b * b)
+            ratio = b * over_a
+            diag = jnp.where(row_ids == k, a, jnp.where(row_ids == k + 1, c - b * ratio, diag))
+            first_mult = jnp.where(row_ids > k + 1, p * over_a, 0.0)
+            second_mult = jnp.where(row_ids > k + 1, (q - ratio * p) * (a * over_det), 0.0)
+            pair_mult = jnp.where(row_ids == k + 1, ratio, first_mult)
+
+            def step(x):
+                top = x[k : k + 1, :]
+                low = x[k + 1 : k + 2, :] - ratio * top
+                return x - pair_mult * top - second_mult * low
+
+            for j in range(k + 2, STEP):
+                cols[j] = step(cols[j])
+            tiles = [step(t) for t in tiles]
         scale = lax.rsqrt(diag)
         tiles = [t * scale for t in tiles]
         for t, tile in zip(names, tiles):
@@ -92,8 +108,11 @@
     size = symmetric.shape[0]
     rows = lax.broadcasted_iota(jnp.int32, (size, size), 0)
     lanes = lax.broadcasted_iota(jnp.int32, (size, size), 1)
-    work[:, :size] = symmetric
-    work[:, size:] = jnp.where(rows == lanes, 1.0, 0.0).astype(F32)
+    diagonal = jnp.where(rows == lanes, symmetric, 0.0)
+    down = lax.rsqrt(jnp.sum(diagonal, axis=1, keepdims=True))
+    along = lax.rsqrt(jnp.sum(diagonal, axis=0, keepdims=True))
+    work[:, :size] = symmetric * down * along
+    work[:, size:] = jnp.where(rows == lanes, down, 0.0)
     inverse[...] = jnp.zeros_like(inverse)
 
 

time: 78.3 us -> 78.6 us (level)
  no operation moved by 1% of the time
where the time goes in v3:
time: 78.6 us; the launch traced here: 78.4 us
  Pallas kernels  72.5 us (92%)
  local copies, waits for them, and re-layouts  5.28 us (7%)
    pallas_call x1, Pallas kernels, body(): pl.pallas_call(functools.partial(kernel, pair_count), out_shape=jax.Shape...  72.5 us
    gather x1, local copies, waits for them, and re-layouts, body(): share = lax.dynamic_slice_in_dim(columns[local], vec * quarter, quarter, 1)  2.19 us
    unnamed x7, local copies, waits for them, and re-layouts  2.08 us

profile of v3, /device:TPU:25, one launch (start us, length us, event | category | flops | bytes accessed | tf_op | source)
XLA Modules:
  0.0 78.4 jit_solution(17940163512427653268)
XLA Ops:
  0.0 0.0 copy-start.2
  0.0 0.7 copy-done.2
  0.7 0.2 convert_reduce_fusion
  1.0 0.2 select_reduce_fusion
  1.2 0.1 reshape.57
  1.3 0.1 copy.5.pos_ref
  1.4 0.0 copy-start.1
  1.4 2.2 %gather_fusion.1 = f32[128,512]{1,0:T(8,128)S(1)} fusion(f32[512,512]{1,0:T(8,128)} %cols_ref.1, s32[1024]{0:T(1024)S(1)} %pad_clamp_fusion), kind=kCustom, calls=%fused_computation.1 | custom fusion | bytes 524800 | tf_op jit(solution)/shard_map/gather | solution.py:327
  3.7 0.0 copy-done.1
  3.7 0.0 copy-start
  3.7 0.8 gather_fusion
  4.5 0.4 copy-done
  4.9 72.5 %shard_map.41 = f32[512,512]{1,0:T(8,128)S(1)} custom-call(f32[2,64,640]{2,1,0:T(8,128)S(1)} %bitcast.4, s32[2,256,1]{2,1,0:T(8,128)S(1)} %copy.5.pos_ref, f32[512,512]{1,0:T(8,128)S(1)} %copy-done.1, f32[512,512]{1,0:T(8,128)S(1)} %copy-done), custom_call_target="tpu_custom_call" | custom-call | tf_op jit(solution)/shard_map/pallas_call | solution.py:356
  77.4 1.0 %copy.7 = f32[512,512]{1,0:T(8,128)} copy(f32[512,512]{1,0:T(8,128)S(1)} %shard_map.41) | data formatting | bytes 2097152
  (8 shorter events, 0.1 us)
Async XLA Ops:
  0.0 0.7 copy-start.2
  1.4 2.2 %copy-start.1 = (f32[512,512]{1,0:T(8,128)S(1)}, f32[512,512]{1,0:T(8,128)}, u32[]{:S(2)}) copy-start(f32[512,512]{1,0:T(8,128)} %prev_ref.1) | copy-start | bytes 3145732
  3.7 1.2 %copy-start = (f32[512,512]{1,0:T(8,128)S(1)}, f32[512,512]{1,0:T(8,128)}, u32[]{:S(2)}) copy-start(f32[512,512]{1,0:T(8,128)} %cols_ref.1) | copy-start | bytes 3145732

commit v4 on v3

--- a/solution.py
+++ b/solution.py
@@ -119,7 +119,7 @@
 def kernel(
     pair_count, sent_ref, pos_ref, prev_ref, cols_ref, out_ref,
     table, p_high, p_low,
-    x1, a1, b1, f1, x2, a2, b2, f2, x3, a3, b3, f3,
+    x1, a1, b1, f1, x2, a2, b2, f2, x3, a3, b3, f3, x4, a4, b4, f4,
     work1, inv1, work2, inv2,
     z_send, z_recv, x_send, x_recv, r_send, r_recv,
 ):
@@ -254,14 +254,19 @@
     rows0 = (p_high[0], p_low[0])
     x1[...] = place_share(share, width) - dot_nt(rows0, rows0)
     stage_a(0, x1, a1).start()
+    own = split2(prev_ref[...])
+    x3[...] = dot_nt(own, rows0)
     a_to_b(0, x1, a1, b1)
+    stage_a(2, x3, a3).start()
     forward(1)
     b_to_c(0, x1, b1, f1)
+    a_to_b(2, x3, a3, b3)
     stage_c_arrival(0, f1).wait_recv()
 
     block = f1[...]
     set_work(work1, inv1, 0.5 * (block + block.T))
     band = eliminate(work1, inv1, 0, 4, start_band(work1))
+    band = eliminate(work1, inv1, 1, 4, band)
 
     finish_gather(1)
     share = ordered(1)
@@ -271,38 +276,41 @@
     x2[...] = place_share(share, 2 * width) - known
     stage_a(1, x2, a2).start()
     own = split2(prev_ref[...])
-    x3[:, :width] = dot_nt(own, rows0)
-    x3[:, width:] = dot_nt(own, rows1)
-    stage_a(2, x3, a3).start()
+    x4[...] = dot_nt(own, rows1)
     a_to_b(1, x2, a2, b2)
-    band = eliminate(work1, inv1, 1, 4, band)
-    a_to_b(2, x3, a3, b3)
+    b_to_c(2, x3, b3, f3)
+    stage_a(3, x4, a4).start()
     band = eliminate(work1, inv1, 2, 4, band)
+    band = eliminate(work1, inv1, 3, 4, band)
     b_to_c(1, x2, b2, f2)
-    band = eliminate(work1, inv1, 3, 4, band)
+    a_to_b(3, x4, a4, b4)
+    inverse1 = split2(inv1[...])
+    stage_c_arrival(2, f3).wait_recv()
     stage_c_arrival(1, f2).wait_recv()
 
-    inverse1 = split2(inv1[...])
     cross = split2(dot_nt(split2(f2[:, :width]), inverse1))
     block = f2[:, width:] - dot_nt(cross, cross)
     set_work(work2, inv2, 0.5 * (block + block.T))
     band = eliminate(work2, inv2, 0, 4, start_band(work2))
+    new1 = dot_nt(split2(cols_ref[:, :width] - f3[...]), inverse1)
+    out_ref[:, :width] = new1
     band = eliminate(work2, inv2, 1, 4, band)
-    b_to_c(2, x3, b3, f3)
+    rest = cols_ref[:, width:] - dot_nt(split2(new1), cross)
     band = eliminate(work2, inv2, 2, 4, band)
-    stage_c_arrival(2, f3).wait_recv()
-    new1 = dot_nt(split2(cols_ref[:, :width] - f3[:, :width]), inverse1)
-    out_ref[:, :width] = new1
-    rest = cols_ref[:, width:] - f3[:, width:] - dot_nt(split2(new1), cross)
+    b_to_c(3, x4, b4, f4)
     band = eliminate(work2, inv2, 3, 4, band)
-    out_ref[:, width:] = dot_nt(split2(rest), split2(inv2[...]))
-
+    stage_c_arrival(3, f4).wait_recv()
+    out_ref[:, width:] = dot_nt(split2(rest - f4[...]), split2(inv2[...]))
+
+    reductions = (
+        (x1, a1, b1, f1), (x2, a2, b2, f2), (x3, a3, b3, f3), (x4, a4, b4, f4),
+    )
     for c in range(panels):
         for d in range(1, outer):
             z_copy(c, d).wait_send()
         for d in range(outer):
             x_copy(c, d).wait_send()
-    for n, (x, a, b, f) in enumerate(((x1, a1, b1, f1), (x2, a2, b2, f2), (x3, a3, b3, f3))):
+    for n, (x, a, b, f) in enumerate(reductions):
         stage_a(n, x, a).wait_send()
         stage_b(n, x, b).wait_send()
         stage_c(n, f).wait_send()
@@ -342,15 +350,16 @@
         vmem(panels, width, depth, dtype=BF16),
         *reduced(width, width),
         *reduced(width, 2 * width),
-        *reduced(slab_rows, 2 * width),
+        *reduced(slab_rows, width),
+        *reduced(slab_rows, width),
         vmem(width, 2 * width), vmem(width, width),
         vmem(width, 2 * width), vmem(width, width),
         pltpu.SemaphoreType.DMA((panels, outer)),
         pltpu.SemaphoreType.DMA((panels, outer)),
         pltpu.SemaphoreType.DMA((panels, outer)),
         pltpu.SemaphoreType.DMA((panels, outer)),
-        pltpu.SemaphoreType.DMA((3, 3)),
-        pltpu.SemaphoreType.DMA((3, 3)),
+        pltpu.SemaphoreType.DMA((4, 3)),
+        pltpu.SemaphoreType.DMA((4, 3)),
     ]
     whole = pl.BlockSpec(memory_space=pltpu.VMEM)
     return pl.pallas_call(

time: 78.6 us -> 72.5 us (0.922)
  Pallas kernels: 72.5 us -> 66.5 us
    pallas_call x1, Pallas kernels: 72.5 us -> 66.5 us  [body(): pl.pallas_call(functools.partial(kernel, pair_count), out_shape=jax.Shape...]
where the time goes in v4:
time: 72.5 us; the launch traced here: 72.4 us
  Pallas kernels  66.5 us (92%)
  local copies, waits for them, and re-layouts  5.28 us (7%)
    pallas_call x1, Pallas kernels, body(): pl.pallas_call(functools.partial(kernel, pair_count), out_shape=jax.Shape...  66.5 us
    gather x1, local copies, waits for them, and re-layouts, body(): share = lax.dynamic_slice_in_dim(columns[local], vec * quarter, quarter, 1)  2.19 us
    unnamed x7, local copies, waits for them, and re-layouts  2.08 us

profile of v4, /device:TPU:25, one launch (start us, length us, event | category | flops | bytes accessed | tf_op | source)
XLA Modules:
  0.0 72.4 jit_solution(1137729080100288569)
XLA Ops:
  0.0 0.0 copy-start.2
  0.0 0.7 copy-done.2
  0.7 0.2 convert_reduce_fusion
  1.0 0.2 select_reduce_fusion
  1.2 0.1 reshape.57
  1.3 0.1 copy.5.pos_ref
  1.4 0.0 copy-start.1
  1.4 2.2 %gather_fusion.1 = f32[128,512]{1,0:T(8,128)S(1)} fusion(f32[512,512]{1,0:T(8,128)} %cols_ref.1, s32[1024]{0:T(1024)S(1)} %pad_clamp_fusion), kind=kCustom, calls=%fused_computation.1 | custom fusion | bytes 524800 | tf_op jit(solution)/shard_map/gather | solution.py:335
  3.7 0.0 copy-done.1
  3.7 0.0 copy-start
  3.7 0.8 %gather_fusion = f32[128,512]{1,0:T(8,128)S(1)} fusion(f32[512,512]{1,0:T(8,128)S(1)} %copy-done.1, s32[1024]{0:T(1024)S(1)} %pad_clamp_fusion), kind=kCustom, calls=%fused_computation | custom fusion | bytes 524800 | tf_op jit(solution)/shard_map/gather | solution.py:336
  4.5 0.4 copy-done
  4.9 66.5 %shard_map.41 = f32[512,512]{1,0:T(8,128)S(1)} custom-call(f32[2,64,640]{2,1,0:T(8,128)S(1)} %bitcast.4, s32[2,256,1]{2,1,0:T(8,128)S(1)} %copy.5.pos_ref, f32[512,512]{1,0:T(8,128)S(1)} %copy-done.1, f32[512,512]{1,0:T(8,128)S(1)} %copy-done), custom_call_target="tpu_custom_call" | custom-call | tf_op jit(solution)/shard_map/pallas_call | solution.py:365
  71.4 1.0 %copy.7 = f32[512,512]{1,0:T(8,128)} copy(f32[512,512]{1,0:T(8,128)S(1)} %shard_map.41) | data formatting | bytes 2097152
  (8 shorter events, 0.1 us)
Async XLA Ops:
  0.0 0.7 copy-start.2
  1.4 2.2 %copy-start.1 = (f32[512,512]{1,0:T(8,128)S(1)}, f32[512,512]{1,0:T(8,128)}, u32[]{:S(2)}) copy-start(f32[512,512]{1,0:T(8,128)} %prev_ref.1) | copy-start | bytes 3145732
  3.7 1.2 %copy-start = (f32[512,512]{1,0:T(8,128)S(1)}, f32[512,512]{1,0:T(8,128)}, u32[]{:S(2)}) copy-start(f32[512,512]{1,0:T(8,128)} %cols_ref.1) | copy-start | bytes 3145732
